TPU v7x, 256 devices: a whole 4x4x8 slice. The times are simulated.
256 devices in a mesh: row: 16 (over x, y_hi, core), col: 16 (over z, y_lo).
Axes of the slice: x: 4, y: 4 (y_hi: 2, y_lo: 2; y = y_hi * 2 + y_lo), z: 8, core: 2. Of those that a mesh axis runs over, the one named last changes fastest.
Arguments:
- grad_iter: bfloat16 [7168, 9216], P('row', 'col'), may hold values from -0.02490811 to 0.02490811
Outputs:
- next_iter: bfloat16 [7168, 9216], P('row', 'col')
All inputs are finite; a program needn't handle non-finite values.
Results may differ from a plain program's by a relative error of at most 0.025.
Values may be sent and summed in bfloat16 or wider, within the bound.
No kernel may reach another device: no remote copies, remote signals or barrier semaphores. Data moves between devices by JAX's collectives and lax.ppermute only.
A program may use at most 128 MiB of HBM per device.

v0:
```python
import jax
import jax.numpy as jnp
from jax import lax
from jax.sharding import PartitionSpec as P

DFF = 9216


linear_coef = 3.4445
cubic_coef = -4.775
quintic_coef = 2.0315


def pair_product(left, right):
    return lax.dot_general(
        left, right, (((1,), (1,)), ((), ())), preferred_element_type=jnp.float32
    )


def per_device(grad_iter):
    row_count = lax.axis_size("row")
    col_count = lax.axis_size("col")
    local_rows = grad_iter.shape[0]
    model_rows = local_rows * row_count
    gram_width = model_rows // col_count
    col_index = lax.axis_index("col")
    columns = lax.all_gather(grad_iter, "row", axis=0, tiled=True)
    partial_value = pair_product(grad_iter, columns)
    gram = lax.psum_scatter(
        partial_value.astype(jnp.bfloat16), "col", scatter_dimension=1, tiled=True
    )
    gram_cols = lax.all_gather(gram, "row", axis=0, tiled=True)
    poly_term = quintic_coef * pair_product(gram, gram_cols)
    offset_cols = col_index * gram_width
    inside = lax.dynamic_slice_in_dim(
        poly_term, offset_cols, gram_width, 1
    ) + cubic_coef * gram.astype(jnp.float32)
    poly_term = lax.dynamic_update_slice_in_dim(poly_term, inside, offset_cols, 1)
    poly_matrix = lax.psum(poly_term.astype(jnp.bfloat16), "col")
    newer = linear_coef * grad_iter.astype(jnp.float32) + jnp.dot(
        poly_matrix, columns, preferred_element_type=jnp.float32
    )
    return (newer * DFF**0.5).astype(jnp.bfloat16)


def solution(mesh):
    placed = (P("row", "col"),)
    return jax.shard_map(
        per_device, mesh=mesh, in_specs=placed, out_specs=P("row", "col"), check_vma=False
    )
```

profile of v0, /device:TPU:40, one launch (start us, length us, event | category | flops | bytes accessed | tf_op | source)
XLA Modules:
  0.0 680.4 jit_solution(2732638048730118474)
XLA Ops:
  6.5 0.0 all-gather.3.cloned.1.call-start
  6.5 0.7 all-gather.3.cloned.1.call-update
  7.3 0.0 reduce-scatter.4.cloned.1.call-start
  7.3 85.5 %all-gather.3.cloned.1.call-done = bf16[7168,576]{1,0:T(8,128)(2,1)} async-done(((bf16[448,576]{1,0:T(8,128)(2,1)}), bf16[7168,576]{1,0:T(8,128)(2,1)}) %all-gather.3.cloned.1.call-update) | async-done | bytes 8257552 | tf_op jit(solution)/shard_map/all_gather | solution.py:27
  92.8 9.6 %convolution_convert_fusion = bf16[448,7168]{1,0:T(8,128)(2,1)} fusion(bf16[448,576]{1,0:T(8,128)(2,1)} %param.1, bf16[7168,576]{1,0:T(8,128)(2,1)} %all-gather.3.cloned.1.call-done), kind=kOutput, calls=%fused_computation.1 | convolution fusion | flops 3702587392 | bytes 15196160 | tf_op jit(solution)/shard_map/dot_general | solution.py:15
  102.4 10.1 %copy.2 = bf16[448,7168]{0,1:T(8,128)(2,1)} copy(bf16[448,7168]{1,0:T(8,128)(2,1)} %convolution_convert_fusion) | data formatting | bytes 12845056
  112.5 0.0 reduce-scatter.4.cloned.1.call-update
  112.5 0.0 all-gather.5.cloned.1.call-start
  112.5 160.7 %reduce-scatter.4.cloned.1.call-done = bf16[448,448]{1,0:T(8,128)(2,1)} async-done(((bf16[7168,448]{1,0:T(8,128)(2,1)}), bf16[448,448]{1,0:T(8,128)(2,1)}) %reduce-scatter.4.cloned.1.call-update) | async-done | bytes 401424
  273.2 2.0 copy.3
  275.2 0.0 all-gather.5.cloned.1.call-update
  275.2 0.0 all-reduce.2.cloned.1.call-start
  275.3 0.0 copy-start.1
  275.3 74.2 %all-gather.5.cloned.1.call-done = bf16[7168,448]{1,0:T(8,128)(2,1)} async-done(((bf16[448,448]{1,0:T(8,128)(2,1)}), bf16[7168,448]{1,0:T(8,128)(2,1)}) %all-gather.5.cloned.1.call-update) | async-done | bytes 6422544 | tf_op jit(solution)/shard_map/all_gather | solution.py:32
  349.4 6.4 convolution_multiply_fusion
  355.8 0.0 copy-start
  355.8 4.6 copy-done
  360.4 0.0 copy-done.1
  360.4 0.3 multiply_add_fusion
  360.7 6.2 dynamic_update_slice.3
  367.0 0.0 copy-start.2
  367.0 8.4 %convert_element_type.18 = bf16[448,7168]{1,0:T(8,128)(2,1)} convert(f32[448,7168]{1,0:T(8,128)} %dynamic_update_slice.3) | non-fusion elementwise | flops 3211264 | bytes 19267584 | tf_op jit(solution)/shard_map/convert_element_type | solution.py:39
  375.3 0.0 all-reduce.2.cloned.1.call-update
  375.4 287.9 %all-reduce.2.cloned.1.call-done = bf16[448,7168]{1,0:T(8,128)(2,1)} async-done(((bf16[448,7168]{1,0:T(8,128)(2,1)}), bf16[448,7168]{1,0:T(8,128)(2,1)}) %all-reduce.2.cloned.1.call-update) | async-done | bytes 6422544 | tf_op jit(solution)/shard_map/psum | solution.py:39
  663.2 0.0 copy-done.2
  663.2 10.6 %fusion.1 = bf16[448,576]{1,0:T(8,128)(2,1)} fusion(bf16[448,7168]{1,0:T(8,128)(2,1)} %all-reduce.2.cloned.1.call-done, bf16[7168,576]{1,0:T(8,128)(2,1)} %all-gather.3.cloned.1.call-done, bf16[448,576]{1,0:T(8,128)(2,1)S(1)} %copy-done.2), kind=kOutput, calls=%fused_computation.4 | convolution fusion | flops 3700666368 | bytes 15712256 | tf_op jit(solution)/shard_map/dot_general | solution.py:40
Async XLA Ops:
  6.5 86.3 %all-gather.3.cloned.1.call-start = ((), (), s32[]{:S(2)}) async-start(), calls=%async_computation.1 | async-start | bytes 9748480 | tf_op jit(solution)/shard_map/all_gather | solution.py:27
  7.3 266.0 %reduce-scatter.4.cloned.1.call-start = ((), (), s32[]{:S(2)}) async-start(), calls=%async_computation.4 | async-start | bytes 7798784
  112.5 236.9 %all-gather.5.cloned.1.call-start = ((), (), s32[]{:S(2)}) async-start(), calls=%async_computation.2 | async-start | bytes 7798784 | tf_op jit(solution)/shard_map/all_gather | solution.py:32
  275.2 388.0 %all-reduce.2.cloned.1.call-start = ((), (), s32[]{:S(2)}) async-start(), calls=%async_computation.3 | async-start | bytes 12845056 | tf_op jit(solution)/shard_map/psum | solution.py:39
  275.3 85.2 %copy-start.1 = (bf16[448,448]{1,0:T(8,128)(2,1)S(1)}, bf16[448,448]{1,0:T(8,128)(2,1)}, u32[]{:S(2)}) copy-start(bf16[448,448]{1,0:T(8,128)(2,1)} %copy.3) | copy-start | bytes 1204228
  355.8 4.6 copy-start
  367.0 296.3 %copy-start.2 = (bf16[448,576]{1,0:T(8,128)(2,1)S(1)}, bf16[448,576]{1,0:T(8,128)(2,1)}, u32[]{:S(2)}) copy-start(bf16[448,576]{1,0:T(8,128)(2,1)} %param.1) | copy-start | bytes 1548292
Sparse Core Ops, SparseCore 0:
  10.0 82.7 all-gather.2
  112.6 160.5 reduce-scatter.3
  275.9 73.4 all-gather.4
  375.5 287.7 all-reduce.1
where the time goes:
time: 681 us; the launch traced here: 680 us
  waiting for transfers between devices  609 us (89%)
  matrix products  26.6 us (4%)
  local copies, waits for them, and re-layouts  22.9 us (3%)
  between operations  13.2 us (2%)
  other arithmetic  8.66 us (1%)
    psum x1, waiting for transfers between devices, per_device(): poly_matrix = lax.psum(poly_term.astype(jnp.bfloat16), 'col')  288 us
    unnamed x5, waiting for transfers between devices  161 us
    all_gather x1, waiting for transfers between devices, per_device(): columns = lax.all_gather(grad_iter, 'row', axis=0, tiled=True)  85.5 us
    all_gather x1, waiting for transfers between devices, per_device(): gram_cols = lax.all_gather(gram, 'row', axis=0, tiled=True)  74.2 us
    unnamed x8, local copies, waits for them, and re-layouts  16.6 us
    dot_general x2, matrix products, pair_product(): lax.dot_general(left, right, (((1,), (1,)), ((), ())), preferred_element_...  16 us
  transfers between devices with their start and end apart: 4, of which 4 were waited for; matrix products, arithmetic and copies ran while one was open for 0% of the time, Pallas kernels for 0%

commit v1 on v0

v1 whole, which is shorter than its diff:
```python
import jax
import jax.numpy as jnp
from jax import lax
from jax.sharding import PartitionSpec as P

DFF = 9216

linear_coef = 3.4445
cubic_coef = -4.775
quintic_coef = 2.0315

AXES = ("row", "col")
NX, NY, NZ, NC = 4, 4, 8, 2


def device_index(x, y, z, c):
    return ((x * 2 + y // 2) * 2 + c) * 16 + z * 2 + y % 2


def every_device():
    return [
        (x, y, z, c)
        for x in range(NX)
        for y in range(NY)
        for z in range(NZ)
        for c in range(NC)
    ]


def permute(value, target):
    pairs = []
    for x, y, z, c in every_device():
        tx, ty, tz, tc = target(x, y, z, c)
        pairs.append(
            (
                device_index(x, y, z, c),
                device_index(tx % NX, ty % NY, tz % NZ, tc % NC),
            )
        )
    return lax.ppermute(value, AXES, pairs)


def z_groups():
    groups = {}
    for x, y, z, c in every_device():
        groups.setdefault((x, y, c), []).append(device_index(x, y, z, c))
    return [groups[key] for key in sorted(groups)]


def along_x(k):
    return lambda x, y, z, c: (x + k, y, z, c)


def along_y(k):
    return lambda x, y, z, c: (x, y + k, z, c)


def along_first(k):
    return lambda x, y, z, c: (x, y + k, z, c) if c == 0 else (x + k, y, z, c)


def along_second(k):
    return lambda x, y, z, c: (x + k, y, z, c) if c == 0 else (x, y + k, z, c)


def other_core(x, y, z, c):
    return (x, y, z, 1 - c)


def swap_layout(x, y, z, c):
    return (x, (y // 2) * 2 + c, z, y % 2)


def dot(left, right, contract):
    return lax.dot_general(
        left, right, (((contract[0],), (contract[1],)), ((), ())),
        preferred_element_type=jnp.float32,
    )


def per_device(grad_iter):
    core = lax.axis_index("row") % NC
    home = permute(grad_iter, swap_layout)
    rows = home.shape[0]
    half = 2 * rows
    b1 = permute(home, along_x(-1))
    a1 = permute(home, along_y(-1))
    b3 = permute(home, along_x(1))
    a3 = permute(home, along_y(1))
    b2 = permute(home, along_x(2))
    a2 = permute(home, along_y(2))
    cols = jnp.concatenate([home, b1, b2, b3], axis=0)
    low = jnp.concatenate([home, a1], axis=0)
    high = jnp.concatenate([a2, a3], axis=0)
    mine = jnp.where(core == 0, low, high)
    other = jnp.where(core == 0, high, low)
    gram_other = dot(other, cols, (1, 1)).astype(jnp.bfloat16)
    received = permute(gram_other, other_core)
    gram_mine = (dot(mine, cols, (1, 1)) + received.astype(jnp.float32)).astype(jnp.bfloat16)
    groups = z_groups()
    part = lax.psum_scatter(
        gram_mine, AXES, scatter_dimension=0, axis_index_groups=groups, tiled=True
    )
    gram_mine = lax.all_gather(
        part, AXES, axis=0, axis_index_groups=groups, tiled=True
    )
    gram_other = permute(gram_mine, other_core)
    gram = jnp.concatenate([gram_mine, gram_other], axis=0)
    lines = jnp.concatenate([mine, other], axis=0)

    def split(value):
        return tuple(value[k * rows:(k + 1) * rows] for k in range(4))

    def first_product(_):
        return split(dot(gram, cols, (1, 0)).astype(jnp.bfloat16))

    def first_product_t(_):
        return split(dot(gram, lines, (0, 0)).astype(jnp.bfloat16))

    terms = lax.cond(core == 0, first_product, first_product_t, 0)
    got = [permute(terms[k], along_first(k)) for k in (1, 3, 2)]
    inner = terms[0].astype(jnp.float32)
    for value in got:
        inner = inner + value.astype(jnp.float32)
    inner_sent = inner.astype(jnp.bfloat16)
    g1 = permute(inner_sent, along_first(-1))
    g3 = permute(inner_sent, along_first(1))
    g2 = permute(inner_sent, along_first(2))

    def second_product(_):
        z = jnp.concatenate([inner_sent, g1, g2, g3], axis=0)
        return split(dot(gram, z, (0, 0)).astype(jnp.bfloat16))

    def second_product_t(_):
        z = jnp.concatenate([inner_sent, g1, g2, g3], axis=0)
        w = split(dot(gram, z, (1, 0)).astype(jnp.bfloat16))
        return (w[2], w[3], w[0], w[1])

    terms = lax.cond(core == 0, second_product, second_product_t, 0)
    got = [permute(terms[k], along_second(k)) for k in (1, 3, 2)]
    outer = terms[0].astype(jnp.float32)
    for value in got:
        outer = outer + value.astype(jnp.float32)
    newer = (
        linear_coef * home.astype(jnp.float32)
        + cubic_coef * inner
        + quintic_coef * outer
    )
    return permute((newer * DFF**0.5).astype(jnp.bfloat16), swap_layout)


def solution(mesh):
    placed = (P("row", "col"),)
    return jax.shard_map(
        per_device, mesh=mesh, in_specs=placed, out_specs=P("row", "col"), check_vma=False
    )
```

time: 681 us -> 292 us (0.43)
  waiting for transfers between devices: 609 us -> 187 us
  starting transfers between devices: 0.13 us -> 39.1 us
    psum x1 -> x0, waiting for transfers between devices: 288 us -> none  [per_device(): poly_matrix = lax.psum(poly_term.astype(jnp.bfloat16), 'col')]
    unnamed x5 -> x2, waiting for transfers between devices: 161 us -> 0.03 us
    all_gather x2 -> x1, waiting for transfers between devices: 160 us -> 47.1 us  [per_device(): lax.all_gather(part, AXES, axis=0, axis_index_groups=groups, tiled=True)]
    ppermute x0 -> x19, waiting for transfers between devices: none -> 93.1 us  [permute(): return lax.ppermute(value, AXES, pairs)]
    reduce_scatter x0 -> x1, waiting for transfers between devices: none -> 46.3 us  [per_device(): lax.psum_scatter(gram_mine, AXES, scatter_dimension=0, axis_index_groups=...]
    ppermute x0 -> x19, starting transfers between devices: none -> 39.1 us  [permute(): return lax.ppermute(value, AXES, pairs)]
    another operation x0 -> x5, local copies, waits for them, and re-layouts: none -> 11 us
    unnamed x8 -> x22, local copies, waits for them, and re-layouts: 16.6 us -> 6.07 us
  transfers between devices with their start and end apart: 4 -> 21, of which waited for: 4 -> 17; matrix products, arithmetic and copies ran while one was open for 0% -> 1% of each run, Pallas kernels for 0% -> 0%
where the time goes in v1:
time: 292 us; the launch traced here: 287 us
  waiting for transfers between devices  187 us (64%)
  starting transfers between devices  39.1 us (13%)
  matrix products  21.4 us (7%)
  local copies, waits for them, and re-layouts  21.3 us (7%)
  between operations  13.7 us (5%)
  other arithmetic  4.89 us (2%)
    ppermute x19, waiting for transfers between devices, permute(): return lax.ppermute(value, AXES, pairs)  93.1 us
    all_gather x1, waiting for transfers between devices, per_device(): lax.all_gather(part, AXES, axis=0, axis_index_groups=groups, tiled=True)  47.1 us
    reduce_scatter x1, waiting for transfers between devices, per_device(): lax.psum_scatter(gram_mine, AXES, scatter_dimension=0, axis_index_groups=...  46.3 us
    ppermute x19, starting transfers between devices, permute(): return lax.ppermute(value, AXES, pairs)  39.1 us
    dot_general x4, matrix products, dot(): lax.dot_general(left, right, (((contract[0],), (contract[1],)), ((), ()))...  21.4 us
    another operation x5, local copies, waits for them, and re-layouts  11 us
    unnamed x22, local copies, waits for them, and re-layouts  6.07 us
  transfers between devices with their start and end apart: 21, of which 17 were waited for; matrix products, arithmetic and copies ran while one was open for 1% of the time, Pallas kernels for 0%

profile of v1, /device:TPU:40, one launch (start us, length us, event | category | flops | bytes accessed | tf_op | source)
XLA Modules:
  0.0 287.4 jit_solution(9045025674555863616)
XLA Ops:
  6.5 1.9 collective-permute-start
  8.5 13.6 %collective-permute-done = bf16[448,576]{1,0:T(8,128)(2,1)S(1)} collective-permute-done((bf16[448,576]{1,0:T(8,128)(2,1)}, bf16[448,576]{1,0:T(8,128)(2,1)S(1)}, u32[]{:S(2)}, u32[]{:S(2)}) %collective-permute-start) | collective-permute-done | bytes 516128 | tf_op jit(solution)/shard_map/ppermute | solution.py:40
  22.0 3.4 %collective-permute-start.2 = (bf16[448,576]{1,0:T(8,128)(2,1)S(1)}, bf16[448,576]{1,0:T(8,128)(2,1)S(1)}, u32[]{:S(2)}, u32[]{:S(2)}) collective-permute-start(bf16[448,576]{1,0:T(8,128)(2,1)S(1)} %collective-permute-done), channel_id=1, source_target_pairs={{0,32},{16,48},{2,34},{18,50},{4,36},{20,52},{6,38},{22,54},{8,40}... | collective-permute-start | bytes 1548296 | tf_op jit(solution)/shard_map/ppermute | solution.py:40
  25.5 2.8 collective-permute-start.4
  28.2 0.8 collective-permute-start.5
  29.0 2.0 collective-permute-start.1
  31.0 0.1 constant_dynamic-update-slice_fusion.7
  31.1 4.1 %collective-permute-done.2 = bf16[448,576]{1,0:T(8,128)(2,1)S(1)} collective-permute-done((bf16[448,576]{1,0:T(8,128)(2,1)S(1)}, bf16[448,576]{1,0:T(8,128)(2,1)S(1)}, u32[]{:S(2)}, u32[]{:S(2)}) %collective-permute-start.2) | collective-permute-done | bytes 516128 | tf_op jit(solution)/shard_map/ppermute | solution.py:40
  35.2 2.1 collective-permute-start.6
  37.3 0.1 constant_dynamic-update-slice_fusion.3
  37.4 6.3 %collective-permute-done.3 = bf16[448,576]{1,0:T(8,128)(2,1)S(1)} collective-permute-done((bf16[448,576]{1,0:T(8,128)(2,1)S(1)}, bf16[448,576]{1,0:T(8,128)(2,1)S(1)}, u32[]{:S(2)}, u32[]{:S(2)}) %collective-permute-start.3) | collective-permute-done | bytes 516128 | tf_op jit(solution)/shard_map/ppermute | solution.py:40
  43.7 0.1 constant_dynamic-update-slice_fusion.2
  43.8 8.6 %collective-permute-done.4 = bf16[448,576]{1,0:T(8,128)(2,1)S(1)} collective-permute-done((bf16[448,576]{1,0:T(8,128)(2,1)S(1)}, bf16[448,576]{1,0:T(8,128)(2,1)S(1)}, u32[]{:S(2)}, u32[]{:S(2)}) %collective-permute-start.4) | collective-permute-done | bytes 516128 | tf_op jit(solution)/shard_map/ppermute | solution.py:40
  52.4 0.1 constant_dynamic-update-slice_fusion.6
  52.5 0.1 constant_dynamic-update-slice_fusion.5
  52.6 0.1 constant_dynamic-update-slice_fusion
  52.7 0.2 broadcast_select_fusion.1
  52.9 3.2 %collective-permute-done.6 = bf16[448,576]{1,0:T(8,128)(2,1)S(1)} collective-permute-done((bf16[448,576]{1,0:T(8,128)(2,1)S(1)}, bf16[448,576]{1,0:T(8,128)(2,1)S(1)}, u32[]{:S(2)}, u32[]{:S(2)}) %collective-permute-start.6) | collective-permute-done | bytes 516128 | tf_op jit(solution)/shard_map/ppermute | solution.py:40
  56.0 0.1 constant_dynamic-update-slice_fusion.4
  56.1 3.0 %convolution_convert_fusion.2 = bf16[896,1792]{1,0:T(8,128)(2,1)S(1)} fusion(bf16[896,576]{1,0:T(8,128)(2,1)S(1)} %get-tuple-element.93, bf16[1792,576]{1,0:T(8,128)(2,1)S(1)} %constant_dynamic-update-slice_fusion.4), kind=kOutput, calls=%fused_computation.23 | convolution fusion | flops 1851293696 | bytes 6307840 | tf_op jit(solution)/shard_map/dot_general | solution.py:75
  59.1 0.1 collective-permute-start.7
  59.2 5.7 %collective-permute-done.7 = bf16[896,1792]{1,0:T(8,128)(2,1)S(1)} collective-permute-done((bf16[896,1792]{1,0:T(8,128)(2,1)S(1)}, bf16[896,1792]{1,0:T(8,128)(2,1)S(1)}, u32[]{:S(2)}, u32[]{:S(2)}) %collective-permute-start.7) | collective-permute-done | bytes 3211296 | tf_op jit(solution)/shard_map/ppermute | solution.py:40
  65.0 4.2 %add_convert_fusion = bf16[896,1792]{1,0:T(8,128)(2,1)} fusion(bf16[896,1792]{1,0:T(8,128)(2,1)S(1)} %collective-permute-done.7, bf16[896,576]{1,0:T(8,128)(2,1)S(1)} %get-tuple-element.92, bf16[1792,576]{1,0:T(8,128)(2,1)S(1)} %constant_dynamic-update-slice_fusion.4), kind=kOutput, calls=%fused_computation.22 | convolution fusion | flops 1854504960 | bytes 9519104 | tf_op jit(solution)/shard_map/dot_general | solution.py:75
  69.1 0.0 all-gather.2.cloned.1.call-start
  69.2 46.3 %reduce-scatter.2.cloned.1.call-done = bf16[112,1792]{1,0:T(8,128)(2,1)} async-done(((bf16[896,1792]{1,0:T(8,128)(2,1)}), bf16[112,1792]{1,0:T(8,128)(2,1)}) %reduce-scatter.2.cloned.1.call-update) | async-done | bytes 401424 | tf_op jit(solution)/shard_map/reduce_scatter | solution.py:101
  115.6 47.1 %all-gather.2.cloned.1.call-done = bf16[896,1792]{1,0:T(8,128)(2,1)} async-done(((bf16[112,1792]{1,0:T(8,128)(2,1)}), bf16[896,1792]{1,0:T(8,128)(2,1)}) %all-gather.2.cloned.1.call-update) | async-done | bytes 3211280 | tf_op jit(solution)/shard_map/all_gather | solution.py:104
  162.7 0.2 pad_maximum_fusion
  162.9 1.7 copy-done.1
  164.6 1.9 constant_dynamic-update-slice_fusion.9
  166.4 2.3 collective-permute-done.8
  168.7 3.8 %constant_dynamic-update-slice_fusion.8 = bf16[1792,1792]{1,0:T(8,128)(2,1)} fusion(bf16[1792,1792]{1,0:T(8,128)(2,1)} %constant_dynamic-update-slice_fusion.9, bf16[896,1792]{1,0:T(8,128)(2,1)} %collective-permute-done.8), kind=kLoop, calls=%fused_computation.38 | loop fusion | bytes 6422528 | tf_op jit(solution)/shard_map/concatenate | solution.py:108
  172.6 7.7 %conditional.5 = (bf16[1792,576]{0,1:T(8,128)(2,1)S(1)}) conditional(s32[]{:T(128)} %convert_element_type.72, (bf16[1792,1792]{1,0:T(8,128)(2,1)}, bf16[1792,576]{1,0:T(8,128)(2,1)S(1)}) %tuple.39, (bf16[1792,1792]{1,0:T(8,128)(2,1)}, bf16[1792,576]{1,0:T(8,128)(2,1)}) %tuple.64), branch_computations={%region_1.2_spmd, %region_2.3_spmd} | conditional | flops 3699376128 | bytes 10551304
  172.8 7.5 %fusion.21 = bf16[1792,576]{0,1:T(8,128)(2,1)S(1)} fusion(bf16[1792,1792]{1,0:T(8,128)(2,1)} %get-tuple-element.59, bf16[1792,576]{1,0:T(8,128)(2,1)} %get-tuple-element.60), kind=kOutput, calls=%fused_computation.42 | convolution fusion | flops 3699376128 | bytes 10551296 | tf_op jit(solution)/shard_map/cond/branch_1_fun/dot_general | solution.py:75
  180.3 1.4 copy-done.6
  181.7 3.1 %copy.2 = bf16[1792,576]{1,0:T(8,128)(2,1)S(1)} copy(bf16[1792,576]{0,1:T(8,128)(2,1)} %copy-done.6) | data formatting | bytes 4128768 | tf_op jit(solution)/shard_map/conditional
  184.8 0.1 fusion.19
  185.0 1.6 collective-permute-start.9
  186.5 1.1 collective-permute-start.11
  187.6 2.1 collective-permute-start.10
  189.8 5.0 %collective-permute-done.9 = bf16[448,576]{1,0:T(8,128)(2,1)S(1)} collective-permute-done((bf16[448,576]{1,0:T(8,128)(2,1)S(1)}, bf16[448,576]{1,0:T(8,128)(2,1)S(1)}, u32[]{:S(2)}, u32[]{:S(2)}) %collective-permute-start.9) | collective-permute-done | bytes 516128 | tf_op jit(solution)/shard_map/ppermute | solution.py:40
  194.7 3.1 %collective-permute-done.11 = bf16[448,576]{1,0:T(8,128)(2,1)S(1)} collective-permute-done((bf16[448,576]{1,0:T(8,128)(2,1)S(1)}, bf16[448,576]{1,0:T(8,128)(2,1)S(1)}, u32[]{:S(2)}, u32[]{:S(2)}) %collective-permute-start.11) | collective-permute-done | bytes 516128 | tf_op jit(solution)/shard_map/ppermute | solution.py:40
  197.8 5.7 %collective-permute-done.10 = bf16[448,576]{1,0:T(8,128)(2,1)S(1)} collective-permute-done((bf16[448,576]{1,0:T(8,128)(2,1)S(1)}, bf16[448,576]{1,0:T(8,128)(2,1)S(1)}, u32[]{:S(2)}, u32[]{:S(2)}) %collective-permute-start.10) | collective-permute-done | bytes 516128 | tf_op jit(solution)/shard_map/ppermute | solution.py:40
  203.5 0.3 fusion.18
  203.8 1.1 collective-permute-start.14
  204.9 11.2 %collective-permute-start.13 = (bf16[448,576]{1,0:T(8,128)(2,1)S(1)}, bf16[448,576]{1,0:T(8,128)(2,1)S(1)}, u32[]{:S(2)}, u32[]{:S(2)}) collective-permute-start(bf16[448,576]{1,0:T(8,128)(2,1)S(1)} %fusion.18), channel_id=1, source_target_pairs={{0,32},{16,144},{2,34},{18,146},{4,36},{20,148},{6,38},{22,150},{8... | collective-permute-start | bytes 1548296 | tf_op jit(solution)/shard_map/ppermute | solution.py:40
  216.1 2.0 collective-permute-start.12
  218.0 8.2 %collective-permute-done.13 = bf16[448,576]{1,0:T(8,128)(2,1)S(1)} collective-permute-done((bf16[448,576]{1,0:T(8,128)(2,1)S(1)}, bf16[448,576]{1,0:T(8,128)(2,1)S(1)}, u32[]{:S(2)}, u32[]{:S(2)}) %collective-permute-start.13) | collective-permute-done | bytes 516128 | tf_op jit(solution)/shard_map/ppermute | solution.py:40
  226.2 5.7 %collective-permute-done.12 = bf16[448,576]{1,0:T(8,128)(2,1)S(1)} collective-permute-done((bf16[448,576]{1,0:T(8,128)(2,1)S(1)}, bf16[448,576]{1,0:T(8,128)(2,1)S(1)}, u32[]{:S(2)}, u32[]{:S(2)}) %collective-permute-start.12) | collective-permute-done | bytes 516128 | tf_op jit(solution)/shard_map/ppermute | solution.py:40
  231.9 10.0 %conditional.6 = (bf16[448,576]{0,1:T(8,128)(2,1)}, bf16[448,576]{0,1:T(8,128)(2,1)}, bf16[448,576]{0,1:T(8,128)(2,1)}, f32[448,576]{1,0:T(8,128)}) conditional(s32[]{:T(128)} %convert_element_type.72, (bf16[448,576]{1,0:T(8,128)(2,1)S(1)}, bf16[448,576]{1,0:T(8,128)(2,1)S(1)}, bf16[448,576]{1,0:T(8,128)(2,1)S(1)}, bf16[448,576]{1,0:T(8,128)(2,1)S(1)}, ...), branch_computations={%region_3.4_spmd, %region_4.5_spmd} | conditional | flops 3708923904 | bytes 17260576
  232.0 6.8 %fusion.9 = bf16[1792,576]{0,1:T(8,128)(2,1)S(1)} fusion(bf16[1792,1792]{1,0:T(8,128)(2,1)} %get-tuple-element.70, bf16[448,576]{1,0:T(8,128)(2,1)S(1)} %get-tuple-element.69, bf16[448,576]{1,0:T(8,128)(2,1)S(1)} %get-tuple-element.68, bf16[448,576]{1,0:T(8,128)(2,1)S(1)} %get-tuple-element.67, bf16[448,576]{1,0:T(8,128)(2,1)S(1)} %get-tuple-element.66), kind=kOutput, calls=%fused_computation.12 | convolution fusion | flops 3708665856 | bytes 10551296 | tf_op jit(solution)/shard_map/cond/branch_1_fun/dot_general | solution.py:75
  238.8 1.8 slice_convert_fusion.1
  240.6 1.4 copy.8
  242.0 2.2 copy.3
  244.2 2.1 copy.5
  246.3 2.1 copy.6
  248.5 3.0 %collective-permute-start.17 = (bf16[448,576]{1,0:T(8,128)(2,1)}, bf16[448,576]{1,0:T(8,128)(2,1)S(1)}, u32[]{:S(2)}, u32[]{:S(2)}) collective-permute-start(bf16[448,576]{1,0:T(8,128)(2,1)} %copy.6), channel_id=1, source_target_pairs={{0,128},{16,48},{2,130},{18,50},{4,132},{20,52},{6,134},{22,54},{8... | collective-permute-start | bytes 1548296 | tf_op jit(solution)/shard_map/ppermute | solution.py:40
  251.4 1.2 collective-permute-start.16
  252.6 0.8 collective-permute-start.15
  253.5 6.5 %collective-permute-done.17 = bf16[448,576]{1,0:T(8,128)(2,1)S(1)} collective-permute-done((bf16[448,576]{1,0:T(8,128)(2,1)}, bf16[448,576]{1,0:T(8,128)(2,1)S(1)}, u32[]{:S(2)}, u32[]{:S(2)}) %collective-permute-start.17) | collective-permute-done | bytes 516128 | tf_op jit(solution)/shard_map/ppermute | solution.py:40
  260.0 6.1 %collective-permute-done.16 = bf16[448,576]{1,0:T(8,128)(2,1)S(1)} collective-permute-done((bf16[448,576]{1,0:T(8,128)(2,1)}, bf16[448,576]{1,0:T(8,128)(2,1)S(1)}, u32[]{:S(2)}, u32[]{:S(2)}) %collective-permute-start.16) | collective-permute-done | bytes 516128 | tf_op jit(solution)/shard_map/ppermute | solution.py:40
  266.1 2.4 multiply_convert_fusion
  268.5 1.9 collective-permute-start.18
  270.4 9.1 %collective-permute-done.18 = bf16[448,576]{1,0:T(8,128)(2,1)S(1)} collective-permute-done((bf16[448,576]{1,0:T(8,128)(2,1)S(1)}, bf16[448,576]{1,0:T(8,128)(2,1)S(1)}, u32[]{:S(2)}, u32[]{:S(2)}) %collective-permute-start.18) | collective-permute-done | bytes 516128 | tf_op jit(solution)/shard_map/ppermute | solution.py:40
  279.5 0.8 copy.26
  (23 shorter events, 0.1 us)
Async XLA Ops:
  6.5 109.0 %reduce-scatter.2.cloned.1.call-start = ((), (), s32[]{:S(2)}) async-start(), calls=%async_computation.1 | async-start | bytes 3612672 | tf_op jit(solution)/shard_map/reduce_scatter | solution.py:101
  6.5 15.5 %collective-permute-start = (bf16[448,576]{1,0:T(8,128)(2,1)}, bf16[448,576]{1,0:T(8,128)(2,1)S(1)}, u32[]{:S(2)}, u32[]{:S(2)}) collective-permute-start(bf16[448,576]{1,0:T(8,128)(2,1)} %param.5), channel_id=1, source_target_pairs={{0,0},{16,1},{2,2},{18,3},{4,4},{20,5},{6,6},{22,7},{8,8},{24,9},{... | collective-permute-start | bytes 1548296 | tf_op jit(solution)/shard_map/ppermute | solution.py:40
  22.0 30.4 %copy-start.2 = (bf16[448,576]{1,0:T(8,128)(2,1)}, bf16[448,576]{1,0:T(8,128)(2,1)S(1)}, u32[]{:S(2)}) copy-start(bf16[448,576]{1,0:T(8,128)(2,1)S(1)} %collective-permute-done) | copy-start | bytes 1548292
  22.0 13.2 %collective-permute-start.2 = (bf16[448,576]{1,0:T(8,128)(2,1)S(1)}, bf16[448,576]{1,0:T(8,128)(2,1)S(1)}, u32[]{:S(2)}, u32[]{:S(2)}) collective-permute-start(bf16[448,576]{1,0:T(8,128)(2,1)S(1)} %collective-permute-done), channel_id=1, source_target_pairs={{0,32},{16,48},{2,34},{18,50},{4,36},{20,52},{6,38},{22,54},{8,40}... | collective-permute-start | bytes 1548296 | tf_op jit(solution)/shard_map/ppermute | solution.py:40
  25.5 18.2 %collective-permute-start.3 = (bf16[448,576]{1,0:T(8,128)(2,1)S(1)}, bf16[448,576]{1,0:T(8,128)(2,1)S(1)}, u32[]{:S(2)}, u32[]{:S(2)}) collective-permute-start(bf16[448,576]{1,0:T(8,128)(2,1)S(1)} %collective-permute-done), channel_id=1, source_target_pairs={{0,1},{16,17},{2,3},{18,19},{4,5},{20,21},{6,7},{22,23},{8,9},{24,... | collective-permute-start | bytes 1548296 | tf_op jit(solution)/shard_map/ppermute | solution.py:40
  25.5 26.9 %collective-permute-start.4 = (bf16[448,576]{1,0:T(8,128)(2,1)S(1)}, bf16[448,576]{1,0:T(8,128)(2,1)S(1)}, u32[]{:S(2)}, u32[]{:S(2)}) collective-permute-start(bf16[448,576]{1,0:T(8,128)(2,1)S(1)} %collective-permute-done), channel_id=1, source_target_pairs={{0,192},{16,208},{2,194},{18,210},{4,196},{20,212},{6,198},{22,214... | collective-permute-start | bytes 1548296 | tf_op jit(solution)/shard_map/ppermute | solution.py:40
  28.2 24.2 %collective-permute-start.5 = (bf16[448,576]{1,0:T(8,128)(2,1)S(1)}, bf16[448,576]{1,0:T(8,128)(2,1)S(1)}, u32[]{:S(2)}, u32[]{:S(2)}) collective-permute-start(bf16[448,576]{1,0:T(8,128)(2,1)S(1)} %collective-permute-done), channel_id=1, source_target_pairs={{0,128},{16,144},{2,130},{18,146},{4,132},{20,148},{6,134},{22,150... | collective-permute-start | bytes 1548296 | tf_op jit(solution)/shard_map/ppermute | solution.py:40
  29.0 23.5 %collective-permute-start.1 = (bf16[448,576]{1,0:T(8,128)(2,1)S(1)}, bf16[448,576]{1,0:T(8,128)(2,1)S(1)}, u32[]{:S(2)}, u32[]{:S(2)}) collective-permute-start(bf16[448,576]{1,0:T(8,128)(2,1)S(1)} %collective-permute-done), channel_id=1, source_target_pairs={{0,33},{16,49},{2,35},{18,51},{4,37},{20,53},{6,39},{22,55},{8,41}... | collective-permute-start | bytes 1548296 | tf_op jit(solution)/shard_map/ppermute | solution.py:40
  35.2 20.8 %collective-permute-start.6 = (bf16[448,576]{1,0:T(8,128)(2,1)S(1)}, bf16[448,576]{1,0:T(8,128)(2,1)S(1)}, u32[]{:S(2)}, u32[]{:S(2)}) collective-permute-start(bf16[448,576]{1,0:T(8,128)(2,1)S(1)} %collective-permute-done), channel_id=1, source_target_pairs={{0,64},{16,80},{2,66},{18,82},{4,68},{20,84},{6,70},{22,86},{8,72}... | collective-permute-start | bytes 1548296 | tf_op jit(solution)/shard_map/ppermute | solution.py:40
  56.1 8.8 %copy-start.7 = (bf16[1792,576]{1,0:T(8,128)(2,1)}, bf16[1792,576]{1,0:T(8,128)(2,1)S(1)}, u32[]{:S(2)}) copy-start(bf16[1792,576]{1,0:T(8,128)(2,1)S(1)} %constant_dynamic-update-slice_fusion.4) | copy-start | bytes 6193156
  59.1 5.8 %collective-permute-start.7 = (bf16[896,1792]{1,0:T(8,128)(2,1)S(1)}, bf16[896,1792]{1,0:T(8,128)(2,1)S(1)}, u32[]{:S(2)}, u32[]{:S(2)}) collective-permute-start(bf16[896,1792]{1,0:T(8,128)(2,1)S(1)} %convolution_convert_fusion.2), channel_id=1, source_target_pairs={{0,16},{16,0},{2,18},{18,2},{4,20},{20,4},{6,22},{22,6},{8,24},{24... | collective-permute-start | bytes 9633800 | tf_op jit(solution)/shard_map/ppermute | solution.py:40
  69.1 93.5 %all-gather.2.cloned.1.call-start = ((), (), s32[]{:S(2)}) async-start(), calls=%async_computation.2 | async-start | bytes 3612672 | tf_op jit(solution)/shard_map/all_gather | solution.py:104
  162.7 6.1 %collective-permute-start.8 = (bf16[896,1792]{1,0:T(8,128)(2,1)}, bf16[896,1792]{1,0:T(8,128)(2,1)}, u32[]{:S(2)}, u32[]{:S(2)}) collective-permute-start(bf16[896,1792]{1,0:T(8,128)(2,1)} %all-gather.2.cloned.1.call-done), channel_id=1, source_target_pairs={{0,16},{16,0},{2,18},{18,2},{4,20},{20,4},{6,22},{22,6},{8,24},{24... | collective-permute-start | bytes 9633800 | tf_op jit(solution)/shard_map/ppermute | solution.py:40
  162.7 1.9 copy-start.1
  180.3 1.4 copy-start.6
  185.0 9.8 %collective-permute-start.9 = (bf16[448,576]{1,0:T(8,128)(2,1)S(1)}, bf16[448,576]{1,0:T(8,128)(2,1)S(1)}, u32[]{:S(2)}, u32[]{:S(2)}) collective-permute-start(bf16[448,576]{1,0:T(8,128)(2,1)S(1)} %get-tuple-element.89), channel_id=1, source_target_pairs={{0,1},{16,80},{2,3},{18,82},{4,5},{20,84},{6,7},{22,86},{8,9},{24,... | collective-permute-start | bytes 1548296 | tf_op jit(solution)/shard_map/ppermute | solution.py:40
  186.5 11.3 %collective-permute-start.11 = (bf16[448,576]{1,0:T(8,128)(2,1)S(1)}, bf16[448,576]{1,0:T(8,128)(2,1)S(1)}, u32[]{:S(2)}, u32[]{:S(2)}) collective-permute-start(bf16[448,576]{1,0:T(8,128)(2,1)S(1)} %get-tuple-element.90), channel_id=1, source_target_pairs={{0,32},{16,144},{2,34},{18,146},{4,36},{20,148},{6,38},{22,150},{8... | collective-permute-start | bytes 1548296 | tf_op jit(solution)/shard_map/ppermute | solution.py:40
  187.6 15.9 %collective-permute-start.10 = (bf16[448,576]{1,0:T(8,128)(2,1)S(1)}, bf16[448,576]{1,0:T(8,128)(2,1)S(1)}, u32[]{:S(2)}, u32[]{:S(2)}) collective-permute-start(bf16[448,576]{1,0:T(8,128)(2,1)S(1)} %get-tuple-element.91), channel_id=1, source_target_pairs={{0,33},{16,208},{2,35},{18,210},{4,37},{20,212},{6,39},{22,214},{8... | collective-permute-start | bytes 1548296 | tf_op jit(solution)/shard_map/ppermute | solution.py:40
  194.7 37.2 %copy-start.3 = (bf16[448,576]{1,0:T(8,128)(2,1)}, bf16[448,576]{1,0:T(8,128)(2,1)S(1)}, u32[]{:S(2)}) copy-start(bf16[448,576]{1,0:T(8,128)(2,1)S(1)} %collective-permute-done.9) | copy-start | bytes 1548292
  197.8 34.1 %copy-start.4 = (bf16[448,576]{1,0:T(8,128)(2,1)}, bf16[448,576]{1,0:T(8,128)(2,1)S(1)}, u32[]{:S(2)}) copy-start(bf16[448,576]{1,0:T(8,128)(2,1)S(1)} %collective-permute-done.11) | copy-start | bytes 1548292
  203.5 28.4 %copy-start.5 = (bf16[448,576]{1,0:T(8,128)(2,1)}, bf16[448,576]{1,0:T(8,128)(2,1)S(1)}, u32[]{:S(2)}) copy-start(bf16[448,576]{1,0:T(8,128)(2,1)S(1)} %collective-permute-done.10) | copy-start | bytes 1548292
  203.8 14.2 %collective-permute-start.14 = (bf16[448,576]{1,0:T(8,128)(2,1)S(1)}, bf16[448,576]{1,0:T(8,128)(2,1)S(1)}, u32[]{:S(2)}, u32[]{:S(2)}) collective-permute-start(bf16[448,576]{1,0:T(8,128)(2,1)S(1)} %fusion.18), channel_id=1, source_target_pairs={{0,1},{16,80},{2,3},{18,82},{4,5},{20,84},{6,7},{22,86},{8,9},{24,... | collective-permute-start | bytes 1548296 | tf_op jit(solution)/shard_map/ppermute | solution.py:40
  204.9 21.3 %collective-permute-start.13 = (bf16[448,576]{1,0:T(8,128)(2,1)S(1)}, bf16[448,576]{1,0:T(8,128)(2,1)S(1)}, u32[]{:S(2)}, u32[]{:S(2)}) collective-permute-start(bf16[448,576]{1,0:T(8,128)(2,1)S(1)} %fusion.18), channel_id=1, source_target_pairs={{0,32},{16,144},{2,34},{18,146},{4,36},{20,148},{6,38},{22,150},{8... | collective-permute-start | bytes 1548296 | tf_op jit(solution)/shard_map/ppermute | solution.py:40
  216.1 15.9 %collective-permute-start.12 = (bf16[448,576]{1,0:T(8,128)(2,1)S(1)}, bf16[448,576]{1,0:T(8,128)(2,1)S(1)}, u32[]{:S(2)}, u32[]{:S(2)}) collective-permute-start(bf16[448,576]{1,0:T(8,128)(2,1)S(1)} %fusion.18), channel_id=1, source_target_pairs={{0,33},{16,208},{2,35},{18,210},{4,37},{20,212},{6,39},{22,214},{8... | collective-permute-start | bytes 1548296 | tf_op jit(solution)/shard_map/ppermute | solution.py:40
  242.0 24.1 %copy-start = (f32[448,576]{1,0:T(8,128)S(1)}, f32[448,576]{1,0:T(8,128)}, u32[]{:S(2)}) copy-start(f32[448,576]{1,0:T(8,128)} %get-tuple-element.80) | copy-start | bytes 3096580
  248.5 11.5 %collective-permute-start.17 = (bf16[448,576]{1,0:T(8,128)(2,1)}, bf16[448,576]{1,0:T(8,128)(2,1)S(1)}, u32[]{:S(2)}, u32[]{:S(2)}) collective-permute-start(bf16[448,576]{1,0:T(8,128)(2,1)} %copy.6), channel_id=1, source_target_pairs={{0,128},{16,48},{2,130},{18,50},{4,132},{20,52},{6,134},{22,54},{8... | collective-permute-start | bytes 1548296 | tf_op jit(solution)/shard_map/ppermute | solution.py:40
  251.4 14.7 %collective-permute-start.16 = (bf16[448,576]{1,0:T(8,128)(2,1)}, bf16[448,576]{1,0:T(8,128)(2,1)S(1)}, u32[]{:S(2)}, u32[]{:S(2)}) collective-permute-start(bf16[448,576]{1,0:T(8,128)(2,1)} %copy.5), channel_id=1, source_target_pairs={{0,192},{16,49},{2,194},{18,51},{4,196},{20,53},{6,198},{22,55},{8... | collective-permute-start | bytes 1548296 | tf_op jit(solution)/shard_map/ppermute | solution.py:40
  252.6 13.5 %collective-permute-start.15 = (bf16[448,576]{1,0:T(8,128)(2,1)}, bf16[448,576]{1,0:T(8,128)(2,1)S(1)}, u32[]{:S(2)}, u32[]{:S(2)}) collective-permute-start(bf16[448,576]{1,0:T(8,128)(2,1)} %copy.3), channel_id=1, source_target_pairs={{0,64},{16,17},{2,66},{18,19},{4,68},{20,21},{6,70},{22,23},{8,72}... | collective-permute-start | bytes 1548296 | tf_op jit(solution)/shard_map/ppermute | solution.py:40
  268.5 11.0 %collective-permute-start.18 = (bf16[448,576]{1,0:T(8,128)(2,1)S(1)}, bf16[448,576]{1,0:T(8,128)(2,1)S(1)}, u32[]{:S(2)}, u32[]{:S(2)}) collective-permute-start(bf16[448,576]{1,0:T(8,128)(2,1)S(1)} %multiply_convert_fusion), channel_id=1, source_target_pairs={{0,0},{16,1},{2,2},{18,3},{4,4},{20,5},{6,6},{22,7},{8,8},{24,9},{... | collective-permute-start | bytes 1548296 | tf_op jit(solution)/shard_map/ppermute | solution.py:40
Sparse Core Ops, SparseCore 0:
  69.3 46.2 reduce-scatter.1
  117.3 45.2 all-gather.1
